TPU v7x, 512 devices: a whole 4x8x8 slice. The times are simulated.
512 devices in a mesh: chan: 8 (over x, z_hi), seq: 64 (over y, z_lo, core).
Axes of the slice: x: 4, y: 8, z: 8 (z_hi: 2, z_lo: 4; z = z_hi * 4 + z_lo), core: 2. Of those that a mesh axis runs over, the one named last changes fastest.
Arguments:
- signal: bfloat16 [524288, 1024], P('seq', 'chan'), may hold values from -6 to 6
- cotangent: bfloat16 [524288, 1024], P('seq', 'chan'), may hold values from -6 to 6
- depth_factor: bfloat16 [64, 64], replicated, may hold values from -0.75 to 0.75
- column_factor: bfloat16 [64, 64], replicated, may hold values from -0.75 to 0.75
- row_factor: bfloat16 [128, 128], replicated, may hold values from -0.5 to 0.5
- depth_mask: int32 [4, 4], replicated, may hold values 0 or 1
- column_mask: int32 [4, 4], replicated, may hold values 0 or 1
- row_mask: int32 [8, 8], replicated, may hold values 0 or 1
Outputs:
- grad_depth: float32 [64, 64], replicated
- grad_column: float32 [64, 64], replicated
- grad_row: float32 [128, 128], replicated
Inputs may be any that keep to these rules, and one draw needn't show every extreme that they name: `depth_mask`: entry 1 keeps a 16 x 16 tile of the factor. `column_mask`: entry 1 keeps a 16 x 16 tile of the factor. `row_mask`: entry 1 keeps a 16 x 16 tile of the factor.
All inputs are finite; a program needn't handle non-finite values.
Results may differ from a plain program's by a relative error of at most 0.0055.
Values may be sent and summed in bfloat16 or wider, within the bound.
A program may use at most 64 MiB of HBM per device.

v0:
```python
import math

import jax
import jax.numpy as jnp
from jax import lax
from jax.sharding import PartitionSpec as P

OUTER = 128
MIDDLE = 64
INNER = 64
CHANNELS = 1024
SEQLEN = 524288


def spread_mask(mask, weight):
    factor = weight.shape[0] // mask.shape[0]
    return jnp.repeat(jnp.repeat(mask, factor, axis=0), factor, axis=1)


def masked(weight, mask):
    return jnp.where(spread_mask(mask, weight) == 1, weight, jnp.zeros_like(weight))


def finish(grad, mask, length):
    count = SEQLEN * CHANNELS // length
    scaled = grad * (1.0 / math.sqrt(count))
    return jnp.where(spread_mask(mask, grad) == 1, scaled, jnp.zeros_like(scaled))


def along(weight, field, form):
    return jnp.einsum(form, weight, field, preferred_element_type=jnp.float32).astype(jnp.bfloat16)


def contract(left, right, form):
    return jnp.einsum(form, left, right, preferred_element_type=jnp.float32)


def per_device(
    signal, cotangent, depth_factor, column_factor, row_factor, depth_mask, column_mask, row_mask
):
    w_depth = masked(depth_factor, depth_mask)
    w_column = masked(column_factor, column_mask)
    w_row = masked(row_factor, row_mask)
    width = signal.shape[1]
    local_rows = signal.shape[0] // (MIDDLE * INNER)
    field = signal.reshape(local_rows, MIDDLE, INNER, width)
    upstream = cotangent.reshape(local_rows, MIDDLE, INNER, width)
    first = along(w_depth, field, "pq,ijqc->ijpc")
    gated = (upstream.astype(jnp.float32) * field.astype(jnp.float32)).astype(jnp.bfloat16)
    second = along(w_column, first, "pq,iqkc->ipkc")
    gated_moved, second_moved = (
        lax.all_to_all(gated, "seq", split_axis=1, concat_axis=0, tiled=True),
        lax.all_to_all(second, "seq", split_axis=1, concat_axis=0, tiled=True),
    )
    grad_row = contract(gated_moved, second_moved, "iabc,jabc->ij")
    back_moved = along(w_row, gated_moved, "pi,pabc->iabc")
    back_second = lax.all_to_all(back_moved, "seq", split_axis=0, concat_axis=1, tiled=True)
    grad_column = contract(back_second, first, "iakc,ibkc->ab")
    back_first = along(w_column, back_second, "pq,ipkc->iqkc")
    grad_depth = contract(back_first, field, "ijpc,ijqc->pq")
    grad_row, grad_column, grad_depth = lax.psum(
        (grad_row, grad_column, grad_depth), ("chan", "seq")
    )
    return (
        finish(grad_depth, depth_mask, INNER),
        finish(grad_column, column_mask, MIDDLE),
        finish(grad_row, row_mask, OUTER),
    )


def solution(mesh):
    in_specs = (P("seq", "chan"), P("seq", "chan"), P(), P(), P(), P(), P(), P())
    out_specs = (P(), P(), P())
    return jax.shard_map(
        per_device, mesh=mesh, in_specs=in_specs, out_specs=out_specs, check_vma=False
    )
```

profile of v0, /device:TPU:1, one launch (start us, length us, event | category | flops | bytes accessed | tf_op | source)
XLA Modules:
  0.0 540.9 jit_solution(10218361884296019571)
XLA Ops:
  7.2 3.2 fusion
  10.3 1.6 copy.56
  11.9 0.0 copy-start.8
  11.9 0.0 copy-start.5
  11.9 0.0 copy-start.9
  11.9 0.0 copy-start.6
  11.9 0.0 copy-start
  12.0 14.9 %all-to-all-start = ((bf16[2,64,64,128]{3,2,0,1:T(8,128)(2,1)}), bf16[2,64,64,128]{3,2,0,1:T(8,128)(2,1)}, u32[]{:S(2)}, u32[]{:S(2)}) async-start(bf16[2,64,64,128]{3,2,0,1:T(8,128)(2,1)} %copy.56), calls=%async_computation | async-start | bytes 4194304 | tf_op jit(solution)/shard_map/all_to_all | solution.py:52
  26.9 0.0 copy-done.8
  26.9 0.1 copy.60
  27.0 0.1 broadcast_in_dim.35
  27.1 0.1 eq.43
  27.2 0.0 copy-done.5
  27.2 0.1 copy.61
  27.3 0.0 copy-done.9
  27.3 0.1 copy.53
  27.4 0.1 broadcast_in_dim.30
  27.5 0.1 eq.37
  27.6 0.0 copy-done.6
  27.6 0.1 copy.64
  27.7 0.0 copy-done
  27.7 0.7 convert_bitcast_fusion.1
  28.5 0.0 copy-start.1
  28.5 1.3 copy-done.1
  29.8 1.8 convert_bitcast_fusion
  31.6 2.7 copy.70
  34.3 0.0 copy-start.7
  34.3 0.0 copy-start.4
  34.3 42.7 %all-to-all-done = bf16[2,64,64,128]{3,2,0,1:T(8,128)(2,1)} async-done(((bf16[2,64,64,128]{3,2,0,1:T(8,128)(2,1)}), bf16[2,64,64,128]{3,2,0,1:T(8,128)(2,1)}, u32[]{:S(2)}, u32[]{:S(2)}) %all-to-all-start) | async-done | bytes 2097184 | tf_op jit(solution)/shard_map/all_to_all | solution.py:52
  77.0 7.2 %all-to-all-start.2 = ((bf16[2,64,64,128]{3,2,0,1:T(8,128)(2,1)}), bf16[2,64,64,128]{3,2,0,1:T(8,128)(2,1)}, u32[]{:S(2)}, u32[]{:S(2)}) async-start(bf16[2,64,64,128]{3,2,0,1:T(8,128)(2,1)} %copy.70), calls=%async_computation.2 | async-start | bytes 4194304 | tf_op jit(solution)/shard_map/all_to_all | solution.py:53
  84.1 0.0 copy-done.7
  84.1 0.1 copy.54
  84.2 0.1 broadcast_in_dim.32
  84.3 0.1 eq.40
  84.4 0.0 copy-done.4
  84.4 0.1 copy.55
  84.5 3.8 copy.57
  88.3 0.0 copy-start.3
  88.3 0.7 convert_bitcast_fusion.3
  89.0 0.6 copy-done.3
  89.7 2.7 copy.58
  92.4 41.8 %all-to-all-done.2 = bf16[2,64,64,128]{3,2,0,1:T(8,128)(2,1)} async-done(((bf16[2,64,64,128]{3,2,0,1:T(8,128)(2,1)}), bf16[2,64,64,128]{3,2,0,1:T(8,128)(2,1)}, u32[]{:S(2)}, u32[]{:S(2)}) %all-to-all-start.2) | async-done | bytes 2097184 | tf_op jit(solution)/shard_map/all_to_all | solution.py:53
  134.2 7.3 %all-to-all-start.1 = ((bf16[128,1,64,128]{3,2,1,0:T(8,128)(2,1)}), bf16[128,1,64,128]{3,2,1,0:T(8,128)(2,1)}, u32[]{:S(2)}, u32[]{:S(2)}) async-start(bf16[128,1,64,128]{3,2,1,0:T(8,128)(2,1)} %copy.58), calls=%async_computation.1 | async-start | bytes 4194304 | tf_op jit(solution)/shard_map/all_to_all | solution.py:57
  141.5 0.0 all-reduce.3.cloned.1.call-start
  141.6 4.3 fusion.15
  145.9 0.0 all-reduce.3.cloned.1.call-update
  145.9 0.1 copy.63
  146.0 0.1 copy.72
  146.1 0.1 copy.67
  146.2 280.8 %all-reduce.3.cloned.1.call-done = f32[128,128]{1,0:T(8,128)} async-done(((f32[128,128]{1,0:T(8,128)}), f32[128,128]{1,0:T(8,128)}) %all-reduce.3.cloned.1.call-update) | async-done | bytes 65552 | tf_op jit(solution)/shard_map/psum | solution.py:61
  427.0 1.5 multiply_select_fusion
  428.5 0.0 all-to-all-done.1
  428.5 0.0 copy-start.2
  428.5 3.5 convert_bitcast_fusion.2
  432.0 0.0 copy-done.2
  432.0 4.0 fusion.21
  436.0 2.0 fusion.18
  438.0 94.8 %all-reduce = (f32[64,64]{1,0:T(8,128)S(1)}, f32[64,64]{1,0:T(8,128)S(1)}) all-reduce(f32[64,64]{1,0:T(8,128)S(1)} %fusion.18, f32[64,64]{1,0:T(8,128)S(1)} %fusion.21), channel_id=1, replica_groups=mesh['chan'=8,'seq'=64] {'chan','seq'}, use_global_device_ids=true, to_apply=%region_0.1 | all-reduce | flops 8192 | bytes 65536 | tf_op jit(solution)/shard_map/psum | solution.py:61
  532.8 0.6 multiply_select_fusion.1
  533.4 0.6 multiply_select_fusion.2
  (7 shorter events, 0.0 us)
Async XLA Ops:
  11.9 15.0 %copy-start.8 = (s32[4,4]{1,0:T(4,128)S(1)}, s32[4,4]{1,0:T(4,128)}, u32[]{:S(2)}) copy-start(s32[4,4]{1,0:T(4,128)} %param.14) | copy-start | bytes 196
  11.9 15.2 %copy-start.5 = (bf16[64,64]{1,0:T(8,128)(2,1)S(1)}, bf16[64,64]{1,0:T(8,128)(2,1)}, u32[]{:S(2)}) copy-start(bf16[64,64]{1,0:T(8,128)(2,1)} %param.11) | copy-start | bytes 24580
  11.9 15.3 %copy-start.9 = (s32[4,4]{1,0:T(4,128)S(1)}, s32[4,4]{1,0:T(4,128)}, u32[]{:S(2)}) copy-start(s32[4,4]{1,0:T(4,128)} %param.13) | copy-start | bytes 196
  11.9 15.6 %copy-start.6 = (bf16[64,64]{1,0:T(8,128)(2,1)S(1)}, bf16[64,64]{1,0:T(8,128)(2,1)}, u32[]{:S(2)}) copy-start(bf16[64,64]{1,0:T(8,128)(2,1)} %param.10) | copy-start | bytes 24580
  11.9 15.8 %copy-start = (bf16[8192,128]{1,0:T(8,128)(2,1)S(1)}, bf16[8192,128]{1,0:T(8,128)(2,1)}, u32[]{:S(2)}) copy-start(bf16[8192,128]{1,0:T(8,128)(2,1)} %param.8) | copy-start | bytes 6291460
  12.0 65.0 %all-to-all-start = ((bf16[2,64,64,128]{3,2,0,1:T(8,128)(2,1)}), bf16[2,64,64,128]{3,2,0,1:T(8,128)(2,1)}, u32[]{:S(2)}, u32[]{:S(2)}) async-start(bf16[2,64,64,128]{3,2,0,1:T(8,128)(2,1)} %copy.56), calls=%async_computation | async-start | bytes 4194304 | tf_op jit(solution)/shard_map/all_to_all | solution.py:52
  28.5 1.3 copy-start.1
  34.3 49.8 %copy-start.7 = (s32[8,8]{1,0:T(8,128)S(1)}, s32[8,8]{1,0:T(8,128)}, u32[]{:S(2)}) copy-start(s32[8,8]{1,0:T(8,128)} %param.15) | copy-start | bytes 772
  34.3 50.1 %copy-start.4 = (bf16[128,128]{1,0:T(8,128)(2,1)S(1)}, bf16[128,128]{1,0:T(8,128)(2,1)}, u32[]{:S(2)}) copy-start(bf16[128,128]{1,0:T(8,128)(2,1)} %param.12) | copy-start | bytes 98308
  77.0 57.2 %all-to-all-start.2 = ((bf16[2,64,64,128]{3,2,0,1:T(8,128)(2,1)}), bf16[2,64,64,128]{3,2,0,1:T(8,128)(2,1)}, u32[]{:S(2)}, u32[]{:S(2)}) async-start(bf16[2,64,64,128]{3,2,0,1:T(8,128)(2,1)} %copy.70), calls=%async_computation.2 | async-start | bytes 4194304 | tf_op jit(solution)/shard_map/all_to_all | solution.py:53
  88.3 1.4 copy-start.3
  134.2 294.3 %all-to-all-start.1 = ((bf16[128,1,64,128]{3,2,1,0:T(8,128)(2,1)}), bf16[128,1,64,128]{3,2,1,0:T(8,128)(2,1)}, u32[]{:S(2)}, u32[]{:S(2)}) async-start(bf16[128,1,64,128]{3,2,1,0:T(8,128)(2,1)} %copy.58), calls=%async_computation.1 | async-start | bytes 4194304 | tf_op jit(solution)/shard_map/all_to_all | solution.py:57
  141.5 285.4 %all-reduce.3.cloned.1.call-start = ((), (), s32[]{:S(2)}) async-start(), calls=%async_computation.3 | async-start | bytes 131072 | tf_op jit(solution)/shard_map/psum | solution.py:61
  428.5 3.5 copy-start.2
Sparse Core Ops, SparseCore 0:
  147.9 278.9 all-reduce.2
where the time goes:
time: 541 us
  waiting for transfers between devices  365 us (67%)
  blocking collectives  94.8 us (18%)
  starting transfers between devices  29.5 us (5%)
  matrix products  17 us (3%)
  local copies, waits for them, and re-layouts  14.2 us (3%)
  between operations  14.2 us (3%)
  other arithmetic  5.92 us (1%)
    psum x1, waiting for transfers between devices, per_device(): lax.psum((grad_row, grad_column, grad_depth), ('chan', 'seq'))  281 us
    psum x1, blocking collectives, per_device(): lax.psum((grad_row, grad_column, grad_depth), ('chan', 'seq'))  94.8 us
    all_to_all x1, waiting for transfers between devices, per_device(): lax.all_to_all(gated, 'seq', split_axis=1, concat_axis=0, tiled=True)  42.7 us
    all_to_all x1, waiting for transfers between devices, per_device(): lax.all_to_all(second, 'seq', split_axis=1, concat_axis=0, tiled=True)  41.8 us
    all_to_all x1, starting transfers between devices, per_device(): lax.all_to_all(gated, 'seq', split_axis=1, concat_axis=0, tiled=True)  14.9 us
  transfers between devices with their start and end apart: 4, of which 3 were waited for; matrix products, arithmetic and copies ran while one was open for 4% of the time, Pallas kernels for 0%

commit v1 on v0

v1 whole, which is shorter than its diff:
```python
import functools
import math

import jax
import jax.numpy as jnp
from jax import lax
from jax.experimental import pallas as pl
from jax.experimental.pallas import tpu as pltpu
from jax.sharding import PartitionSpec as P

CHANNELS = 1024
SEQLEN = 524288
MIDDLE = 64
INNER = 64
LANES = 128
X, ZH, Y, ZL, CORES = 4, 2, 8, 4, 2
CHUNK = 16
Y_ORDER = (1, 7, 2, 6, 3, 5, 4, 0)
F32, BF16 = jnp.float32, jnp.bfloat16
MESH = pl.DeviceIdType.MESH


def dot(a, b, contract):
    return lax.dot_general(a, b, ((contract[:1], contract[1:]), ((), ())), preferred_element_type=F32)


def iota(shape, axis):
    return lax.broadcasted_iota(jnp.int32, shape, axis)


def onehot(shape, left, right):
    return jnp.where(left(iota(shape, 0)) == right(iota(shape, 1)), 1.0, 0.0)


def same(value):
    return value


def spread_mask(mask_ref, size):
    tiles = mask_ref.shape[0]
    side = size // tiles
    mask = jnp.where(mask_ref[...] == 1, 1.0, 0.0)
    rows = onehot((size, tiles), lambda r: r // side, same)
    columns = onehot((tiles, size), same, lambda c: c // side)
    return dot(dot(rows, mask, (1, 0)), columns, (1, 0))


def twice(weight):
    size = weight.shape[0]
    rows = onehot((2 * size, size), lambda r: r % size, same).astype(BF16)
    columns = onehot((size, 2 * size), same, lambda c: c % size).astype(BF16)
    full = dot(dot(rows, weight, (1, 0)).astype(BF16), columns, (1, 0))
    return (full * onehot(full.shape, lambda r: r // size, lambda c: c // size)).astype(BF16)


def kernel(
    seqs, outer, chunk,
    signal_hbm, cotangent_hbm, depth_ref, column_ref, row_ref, depth_mask, column_mask, row_mask,
    out_depth, out_column, out_row,
    signal, cotangent, flipped, send_x, send_g, got_x, got_g, first, mixed, second, wide, back,
    w_row_t, w_depth2, w_column2, parts, land_1, land_2, land_3, land_4, sum_1, sum_2, sum_3,
    load_sem, self_sem, send_sem, recv_sem, part_send, part_recv,
):
    jk = MIDDLE * INNER
    chunks = MIDDLE // chunk
    pair = 2 * chunk
    width = 2 * seqs
    ring = ZL * CORES
    chan, me = lax.axis_index("chan"), lax.axis_index("seq")
    x, z_hi = chan // ZH, chan % ZH
    y, inner = me // ring, me % ring
    z_lo, core = inner // CORES, inner % CORES
    z = z_hi * ZL + z_lo
    local_rows = (outer + MIDDLE) // Y

    load_x = pltpu.make_async_copy(signal_hbm, signal, load_sem.at[0])
    load_c = pltpu.make_async_copy(cotangent_hbm, cotangent, load_sem.at[1])
    load_x.start()
    load_c.start()

    def y_peer(step):
        return chan, lax.rem(y + step, Y) * ring + inner

    def z_peer(step):
        there = lax.rem(z + step, ZH * ZL)
        return x * ZH + there // ZL, y * ring + lax.rem(there, ZL) * CORES + core

    def x_peer(step):
        there = lax.rem(x * CORES + core + step, X * CORES)
        return there // CORES * ZH + z_hi, y * ring + z_lo * CORES + lax.rem(there, CORES)

    barrier = pltpu.get_barrier_semaphore()

    @pl.loop(1, seqs)
    def _(step):
        pl.semaphore_signal(barrier, inc=1, device_id=(chan, lax.rem(me + step, seqs)), device_id_type=MESH)

    greeted = seqs - 1
    for away in range(ZL):
        if ZH == 2:
            pl.semaphore_signal(
                barrier, inc=1,
                device_id=(x * ZH + 1 - z_hi, y * ring + away * CORES + core), device_id_type=MESH,
            )
            greeted += 1
    for step in range(1, X):
        for other in range(CORES):
            there = lax.rem(x + step, X) * ZH + z_hi
            pl.semaphore_signal(
                barrier, inc=1, device_id=(there, y * ring + z_lo * CORES + other), device_id_type=MESH
            )
            greeted += 1

    pick = onehot((seqs, width), same, lambda c: c // 2).astype(BF16)
    even = jnp.where(iota((1, width), 1) % 2 == 0, 1.0, 0.0).astype(BF16)
    odd = jnp.where(iota((1, width), 1) % 2 == 1, 1.0, 0.0).astype(BF16)

    def flip(read):
        def body(block, carry):
            value = read(pl.ds(pl.multiple_of(block * INNER, INNER), INNER))
            both = jnp.concatenate([value * even, value * odd], axis=0)
            flipped[pl.ds(pl.multiple_of(block * seqs, seqs), seqs), :] = dot(pick, both, (1, 1))
            return carry

        lax.fori_loop(0, 2 * MIDDLE, body, 0, unroll=8)

    def send(source, target, slot, run):
        def body(turn, carry):
            for place, away in enumerate(Y_ORDER):
                if away >= Y:
                    continue
                step = lax.rem(turn + place + 1, ring)
                to = lax.rem(y + away, Y) * ring + lax.rem(inner + step, ring)

                def go():
                    pltpu.make_async_remote_copy(
                        src_ref=source(to), dst_ref=target(me),
                        send_sem=send_sem.at[slot], recv_sem=recv_sem.at[slot],
                        device_id=(chan, to), device_id_type=MESH,
                    ).start()

                if away == 0:
                    pl.when(step != 0)(go)
                else:
                    go()
            return carry

        lax.fori_loop(0, ring, body, 0)
        return run

    load_x.wait()
    flip(lambda rows: signal[rows, :])

    def pack_x(d, carry):
        send_x[d] = flipped[pl.ds(d, 2 * MIDDLE, stride=seqs), :].astype(BF16)
        return carry

    lax.fori_loop(0, seqs, pack_x, 0, unroll=4)
    pl.semaphore_wait(barrier, greeted)
    send(lambda to: send_x.at[to], lambda at: got_x.at[at], 0, None)
    own_x = pltpu.make_async_copy(send_x.at[me], got_x.at[me], self_sem.at[0])
    own_x.start()

    load_c.wait()
    flip(lambda rows: (cotangent[rows, :].astype(F32) * signal[rows, :].astype(F32)).astype(BF16))
    owns = []
    for part in range(chunks):
        def pack_g(d, carry):
            for i in range(2):
                start = (i * MIDDLE + part * chunk) * seqs + d
                send_g[part, d, i * chunk : (i + 1) * chunk, :] = flipped[
                    pl.ds(start, chunk, stride=seqs), :
                ].astype(BF16)
            return carry

        lax.fori_loop(0, seqs, pack_g, 0, unroll=4)
        send(lambda to: send_g.at[part, to], lambda at: got_g.at[part, at], 1 + part, None)
        own = pltpu.make_async_copy(send_g.at[part, me], got_g.at[part, me], self_sem.at[1 + part])
        own.start()
        owns.append(own)

    keep_row = spread_mask(row_mask, outer)
    keep_column = spread_mask(column_mask, MIDDLE)
    keep_depth = spread_mask(depth_mask, INNER)
    w_row = (row_ref[...].astype(F32) * keep_row).astype(BF16)
    w_row_t[...] = dot(onehot((outer, outer), same, same).astype(BF16), w_row, (1, 1)).astype(BF16)
    w_depth2[...] = twice((depth_ref[...].astype(F32) * keep_depth).astype(BF16))
    w_column2[...] = twice((column_ref[...].astype(F32) * keep_column).astype(BF16))

    def arrived(ref, sem):
        others = ref.at[pl.ds(0, seqs - 1)]
        pltpu.make_async_copy(others, others, sem).wait()

    own_x.wait()
    arrived(got_x, recv_sem.at[0])

    def signal_side(s, carry):
        field = got_x[s]
        one = dot(field, w_depth2[...], (1, 1)).astype(BF16)
        first[s] = one
        two = dot(w_column2[...], jnp.concatenate([field, one], axis=1), (1, 0))
        for part in range(chunks):
            for i in range(2):
                mixed[part, s, i * chunk : (i + 1) * chunk, :] = two[
                    i * MIDDLE + part * chunk : i * MIDDLE + (part + 1) * chunk, :LANES
                ].astype(BF16)
        wide[pl.ds(pl.multiple_of(s * 2 * MIDDLE, 2 * MIDDLE), 2 * MIDDLE), :] = two[:, LANES:]
        return carry

    lax.fori_loop(0, seqs, signal_side, 0, unroll=4)

    def by_column(j, carry):
        second[j] = wide[pl.ds(j, outer, stride=MIDDLE), :].astype(BF16)
        return carry

    lax.fori_loop(0, MIDDLE, by_column, 0, unroll=4)

    grad_row = jnp.zeros((outer, outer), F32)
    grad_depth = jnp.zeros((LANES, LANES), F32)
    group = min(4, seqs)
    for part in range(chunks):
        owns[part].wait()
        arrived(got_g.at[part], recv_sem.at[1 + part])

        def widen(s, carry):
            wide[pl.ds(pl.multiple_of(s * pair, pair), pair), :] = got_g[part, s].astype(F32)
            return carry

        lax.fori_loop(0, seqs, widen, 0, unroll=8)

        def row_side(j, total):
            gated = wide[pl.ds(j, outer, stride=chunk), :].astype(BF16)
            back[pl.ds(j, outer, stride=chunk), :] = dot(w_row_t[...], gated, (1, 0))
            return total + dot(gated, second[part * chunk + j], (1, 1))

        grad_row = lax.fori_loop(0, chunk, row_side, grad_row, unroll=4)

        def back_side(block, carry):
            column, depth = carry
            rows = group * pair
            value = back[pl.ds(pl.multiple_of(block * rows, rows), rows), :].astype(BF16)
            fields = mixed[part, pl.ds(block * group, group)].reshape(rows, LANES)
            depth = depth + dot(value, fields, (0, 0))
            ours, theirs = [], []
            for s in range(group):
                at = s * pair
                ours.append(jnp.concatenate([value[at : at + chunk], value[at + chunk : at + pair]], axis=1))
                one = first[block * group + s]
                theirs.append(jnp.concatenate([one[:MIDDLE], one[MIDDLE:]], axis=1))
            column = column + dot(jnp.concatenate(ours, axis=0), jnp.concatenate(theirs, axis=0), (1, 1))
            return column, depth

        column, grad_depth = lax.fori_loop(
            0, seqs // group, back_side,
            (jnp.zeros((group * chunk, group * MIDDLE), F32), grad_depth), unroll=2,
        )
        piece = jnp.zeros((chunk, MIDDLE), F32)
        for s in range(group):
            piece = piece + column[s * chunk : (s + 1) * chunk, s * MIDDLE : (s + 1) * MIDDLE]
        parts[outer + part * chunk : outer + (part + 1) * chunk, :MIDDLE] = piece
    parts[:outer, :outer] = grad_row
    parts[outer:, MIDDLE:] = grad_depth[:INNER, :INNER] + grad_depth[INNER:, INNER:]

    def exchange(phase, count, peer, source, target):
        copies = []
        for step in range(1, count):
            to = peer(step)
            copy = pltpu.make_async_remote_copy(
                src_ref=source(to), dst_ref=target,
                send_sem=part_send.at[phase], recv_sem=part_recv.at[phase],
                device_id=to, device_id_type=MESH,
            )
            copy.start()
            copies.append(copy)

    def landed(phase, land, count):
        others = land.at[pl.ds(0, count - 1)]
        pltpu.make_async_copy(others, others, part_recv.at[phase]).wait()

    def added(land):
        total = land[0]
        for slot in range(1, land.shape[0]):
            total = total + land[slot]
        return total

    def rows_of(place):
        return pl.ds(pl.multiple_of(place * local_rows, 8), local_rows)

    land_1[y] = parts[rows_of(y), :]
    exchange(0, Y, y_peer, lambda to: parts.at[rows_of(to[1] // ring)], land_1.at[y])
    landed(0, land_1, Y)
    sum_1[...] = added(land_1)
    land_2[z] = sum_1[...]
    exchange(1, ZH * ZL, z_peer, lambda to: sum_1, land_2.at[z])
    landed(1, land_2, ZH * ZL)
    sum_2[...] = added(land_2)
    place = x * CORES + core
    land_3[place] = sum_2[...]
    exchange(2, X * CORES, x_peer, lambda to: sum_2, land_3.at[place])
    landed(2, land_3, X * CORES)
    sum_3[...] = added(land_3)
    land_4[y] = sum_3[...]
    exchange(3, Y, y_peer, lambda to: sum_3, land_4.at[y])
    landed(3, land_4, Y)

    whole = land_4[...].reshape(outer + MIDDLE, LANES)
    inner_count = 1.0 / math.sqrt(SEQLEN * CHANNELS // MIDDLE)
    outer_count = 1.0 / math.sqrt(SEQLEN * CHANNELS // outer)
    out_row[...] = jnp.where(keep_row > 0.5, whole[:outer, :outer] * outer_count, 0.0)
    out_column[...] = jnp.where(keep_column > 0.5, whole[outer:, :MIDDLE] * inner_count, 0.0)
    out_depth[...] = jnp.where(keep_depth > 0.5, whole[outer:, MIDDLE:] * inner_count, 0.0)

    def sent(ref, sem):
        others = ref.at[pl.ds(0, seqs - 1)]
        pltpu.make_async_copy(others, others, sem).wait()

    sent(send_x, send_sem.at[0])
    for part in range(chunks):
        sent(send_g.at[part], send_sem.at[1 + part])
    for phase, (land, count) in enumerate(
        ((land_1, Y), (land_2, ZH * ZL), (land_3, X * CORES), (land_4, Y))
    ):
        others = land.at[pl.ds(0, count - 1)]
        pltpu.make_async_copy(others, others, part_send.at[phase]).wait()


def per_device(
    signal, cotangent, depth_factor, column_factor, row_factor, depth_mask, column_mask, row_mask
):
    seqs = Y * ZL * CORES
    outer = row_factor.shape[0]
    chunk = CHUNK
    chunks = MIDDLE // chunk
    pair = 2 * chunk
    rows, width = signal.shape
    local_rows = (outer + MIDDLE) // Y
    vmem = pl.BlockSpec(memory_space=pltpu.VMEM)
    hbm = pl.BlockSpec(memory_space=pl.ANY)
    return pl.pallas_call(
        functools.partial(kernel, seqs, outer, chunk),
        out_shape=(
            jax.ShapeDtypeStruct((INNER, INNER), F32),
            jax.ShapeDtypeStruct((MIDDLE, MIDDLE), F32),
            jax.ShapeDtypeStruct((outer, outer), F32),
        ),
        in_specs=[hbm, hbm] + [vmem] * 6,
        out_specs=(vmem, vmem, vmem),
        scratch_shapes=[
            pltpu.VMEM((rows, width), BF16),
            pltpu.VMEM((rows, width), BF16),
            pltpu.VMEM((2 * MIDDLE * seqs, LANES), F32),
            pltpu.VMEM((seqs, 2 * MIDDLE, LANES), BF16),
            pltpu.VMEM((chunks, seqs, pair, LANES), BF16),
            pltpu.VMEM((seqs, 2 * MIDDLE, LANES), BF16),
            pltpu.VMEM((chunks, seqs, pair, LANES), BF16),
            pltpu.VMEM((seqs, 2 * MIDDLE, LANES), BF16),
            pltpu.VMEM((chunks, seqs, pair, LANES), BF16),
            pltpu.VMEM((MIDDLE, outer, LANES), BF16),
            pltpu.VMEM((outer * MIDDLE, LANES), F32),
            pltpu.VMEM((outer * chunk, LANES), F32),
            pltpu.VMEM((outer, outer), BF16),
            pltpu.VMEM((LANES, LANES), BF16),
            pltpu.VMEM((LANES, LANES), BF16),
            pltpu.VMEM((outer + MIDDLE, LANES), F32),
            pltpu.VMEM((Y, local_rows, LANES), F32),
            pltpu.VMEM((ZH * ZL, local_rows, LANES), F32),
            pltpu.VMEM((X * CORES, local_rows, LANES), F32),
            pltpu.VMEM((Y, local_rows, LANES), F32),
            pltpu.VMEM((local_rows, LANES), F32),
            pltpu.VMEM((local_rows, LANES), F32),
            pltpu.VMEM((local_rows, LANES), F32),
            pltpu.SemaphoreType.DMA((2,)),
            pltpu.SemaphoreType.DMA((1 + chunks,)),
            pltpu.SemaphoreType.DMA((1 + chunks,)),
            pltpu.SemaphoreType.DMA((1 + chunks,)),
            pltpu.SemaphoreType.DMA((4,)),
            pltpu.SemaphoreType.DMA((4,)),
        ],
        compiler_params=pltpu.CompilerParams(
            collective_id=0, has_side_effects=True, vmem_limit_bytes=48 * 2**20
        ),
        cost_estimate=pl.CostEstimate(flops=1_300_000_000, bytes_accessed=4 * 2**20, transcendentals=0),
    )(signal, cotangent, depth_factor, column_factor, row_factor, depth_mask, column_mask, row_mask)


def solution(mesh):
    in_specs = (P("seq", "chan"), P("seq", "chan"), P(), P(), P(), P(), P(), P())
    out_specs = (P(), P(), P())
    return jax.shard_map(
        per_device, mesh=mesh, in_specs=in_specs, out_specs=out_specs, check_vma=False
    )
```

time: 541 us -> 149 us (0.28)
  waiting for transfers between devices: 365 us -> 0 us
  Pallas kernels: 0 us -> 139 us
  blocking collectives: 94.8 us -> 0 us
  starting transfers between devices: 29.5 us -> 0 us
  matrix products: 17 us -> 0 us
  between operations: 14.2 us -> 0.66 us
  other arithmetic: 5.92 us -> 0 us
    psum x1 -> x0, waiting for transfers between devices: 281 us -> none  [per_device(): lax.psum((grad_row, grad_column, grad_depth), ('chan', 'seq'))]
    pallas_call x0 -> x1, Pallas kernels: none -> 139 us  [per_device(): pl.pallas_call(functools.partial(kernel, seqs, outer, chunk), out_shape=(...]
    psum x1 -> x0, blocking collectives: 94.8 us -> none  [per_device(): lax.psum((grad_row, grad_column, grad_depth), ('chan', 'seq'))]
    all_to_all x3 -> x0, waiting for transfers between devices: 84.5 us -> none  [the longest x1 42.7 us: per_device(): lax.all_to_all(gated, 'seq', split_axis=1, concat_axis=0, tiled=True)]
    all_to_all x3 -> x0, starting transfers between devices: 29.4 us -> none  [the longest x1 14.9 us: per_device(): lax.all_to_all(gated, 'seq', split_axis=1, concat_axis=0, tiled=True)]
    dot_general x7 -> x0, matrix products: 17 us -> none  [the longest x3 10.2 us: contract(): return jnp.einsum(form, left, right, preferred_element_type=jnp.float32)]
    unnamed x23 -> x19, local copies, waits for them, and re-layouts: 2.3 us -> 9.27 us
    convert_element_type x3 -> x0, local copies, waits for them, and re-layouts: 6.96 us -> none  [the longest x2 5.37 us: along(): jnp.einsum(form, weight, field, preferred_element_type=jnp.float32)]
  transfers between devices with their start and end apart: 4 -> 0, of which waited for: 3 -> 0; matrix products, arithmetic and copies ran while one was open for 4% -> 0% of each run, Pallas kernels for 0% -> 0%
where the time goes in v1:
time: 149 us
  Pallas kernels  139 us (93%)
  local copies, waits for them, and re-layouts  9.27 us (6%)
    pallas_call x1, Pallas kernels, per_device(): pl.pallas_call(functools.partial(kernel, seqs, outer, chunk), out_shape=(...  139 us
    unnamed x19, local copies, waits for them, and re-layouts  9.27 us

profile of v1, /device:TPU:1, one launch (start us, length us, event | category | flops | bytes accessed | tf_op | source)
XLA Modules:
  0.0 148.8 jit_solution(9208742748364458906)
XLA Ops:
  0.6 0.0 copy-start
  0.6 1.6 %copy-done = bf16[8192,128]{1,0:T(8,128)(2,1)S(1)} copy-done((bf16[8192,128]{1,0:T(8,128)(2,1)S(1)}, bf16[8192,128]{1,0:T(8,128)(2,1)}, u32[]{:S(2)}) %copy-start) | copy-done | bytes 2097176
  2.2 0.0 copy-start.1
  2.2 1.6 %copy-done.1 = bf16[8192,128]{1,0:T(8,128)(2,1)S(1)} copy-done((bf16[8192,128]{1,0:T(8,128)(2,1)S(1)}, bf16[8192,128]{1,0:T(8,128)(2,1)}, u32[]{:S(2)}) %copy-start.1) | copy-done | bytes 2097176
  3.8 0.0 copy-start.2
  3.8 0.8 copy-done.2
  4.6 0.0 copy-start.3
  4.6 0.7 copy-done.3
  5.3 0.0 copy-start.4
  5.3 0.7 copy-done.4
  6.0 0.0 copy-start.5
  6.0 0.7 copy-done.5
  6.7 0.0 copy-start.6
  6.7 0.7 copy-done.6
  7.4 0.0 copy-start.7
  7.4 0.7 copy-done.7
  8.1 138.9 %shard_map.103 = (f32[64,64]{1,0:T(8,128)S(1)}, f32[64,64]{1,0:T(8,128)S(1)}, f32[128,128]{1,0:T(8,128)S(1)}) custom-call(bf16[8192,128]{1,0:T(8,128)(2,1)S(1)} %copy-done, bf16[8192,128]{1,0:T(8,128)(2,1)S(1)} %copy-done.1, bf16[64,64]{1,0:T(8,128)(2,1)S(1)} %copy-done.3, bf16[64,64]{1,0:T(8,128)(2,1)S(1)} %copy-done.4, bf16[128,128]{1,0:T(8,128)(2,1)S(1)} %copy-done.2, ...), custom_call_target="tpu_custom_call" | custom-call | flops 1300000000 | bytes 4194304 | tf_op jit(solution)/shard_map/pallas_call | solution.py:339
  147.0 0.6 copy.14
  147.6 0.6 copy.15
  148.2 0.6 copy.16
Async XLA Ops:
  0.6 1.6 %copy-start = (bf16[8192,128]{1,0:T(8,128)(2,1)S(1)}, bf16[8192,128]{1,0:T(8,128)(2,1)}, u32[]{:S(2)}) copy-start(bf16[8192,128]{1,0:T(8,128)(2,1)} %signal_hbm.1) | copy-start | bytes 6291460
  2.2 1.6 %copy-start.1 = (bf16[8192,128]{1,0:T(8,128)(2,1)S(1)}, bf16[8192,128]{1,0:T(8,128)(2,1)}, u32[]{:S(2)}) copy-start(bf16[8192,128]{1,0:T(8,128)(2,1)} %cotangent_hbm.1) | copy-start | bytes 6291460
  3.8 0.8 copy-start.2
  4.6 0.7 copy-start.3
  5.3 0.7 copy-start.4
  6.0 0.7 copy-start.5
  6.7 0.7 copy-start.6
  7.4 0.7 copy-start.7

commit v2 on v1

v2 whole, which is shorter than its diff:
```python
import functools
import math

import jax
import jax.numpy as jnp
from jax import lax
from jax.experimental import pallas as pl
from jax.experimental.pallas import tpu as pltpu
from jax.sharding import PartitionSpec as P

CHANNELS = 1024
SEQLEN = 524288
MIDDLE = 64
INNER = 64
LANES = 128
X, ZH, Y, ZL, CORES = 4, 2, 8, 4, 2
PARTS = (16, 16, 16, 8, 8)
Y_ORDER = (1, 7, 2, 6, 3, 5, 4, 0)
FAR_FIRST = (4, 3, 5, 2, 6, 1, 7)
F32, BF16 = jnp.float32, jnp.bfloat16
MESH = pl.DeviceIdType.MESH


def dot(a, b, contract):
    return lax.dot_general(a, b, ((contract[:1], contract[1:]), ((), ())), preferred_element_type=F32)


def iota(shape, axis):
    return lax.broadcasted_iota(jnp.int32, shape, axis)


def onehot(shape, left, right):
    return jnp.where(left(iota(shape, 0)) == right(iota(shape, 1)), 1.0, 0.0)


def same(value):
    return value


def spread_mask(mask, size):
    tiles = mask.shape[0]
    side = size // tiles
    ones = jnp.where(mask == 1, 1.0, 0.0)
    rows = onehot((size, tiles), lambda r: r // side, same)
    columns = onehot((tiles, size), same, lambda c: c // side)
    return dot(dot(rows, ones, (1, 0)), columns, (1, 0))


def twice(weight):
    size = weight.shape[0]
    rows = onehot((2 * size, size), lambda r: r % size, same).astype(BF16)
    columns = onehot((size, 2 * size), same, lambda c: c % size).astype(BF16)
    full = dot(dot(rows, weight, (1, 0)).astype(BF16), columns, (1, 0))
    return (full * onehot(full.shape, lambda r: r // size, lambda c: c // size)).astype(BF16)


def kernel(
    seqs, outer,
    signal_hbm, cotangent_hbm, depth_hbm, column_hbm, row_hbm, depth_mask_hbm, column_mask_hbm, row_mask_hbm,
    out_depth, out_column, out_row,
    signal, cotangent, depth_ref, column_ref, row_ref, depth_mask, column_mask, row_mask,
    flipped, send_x, send_g, got_x, got_g, first, mixed, second, wide, back,
    w_row_t, w_depth2, w_column2, sums, land_1, land_2, land_3, land_4, sum_1, sum_2, sum_3,
    load_sem, self_sem, send_sem, recv_sem, part_send, part_recv,
):
    starts = [sum(PARTS[:part]) for part in range(len(PARTS))]
    width = 2 * seqs
    ring = ZL * CORES
    chan, me = lax.axis_index("chan"), lax.axis_index("seq")
    x, z_hi = chan // ZH, chan % ZH
    y, inner = me // ring, me % ring
    z_lo, core = inner // CORES, inner % CORES
    z = z_hi * ZL + z_lo
    local_rows = (outer + MIDDLE) // (X * CORES)

    loads = [
        pltpu.make_async_copy(source, target, load_sem.at[place])
        for place, (source, target) in enumerate((
            (signal_hbm, signal), (cotangent_hbm, cotangent),
            (depth_hbm, depth_ref), (column_hbm, column_ref), (row_hbm, row_ref),
            (depth_mask_hbm, depth_mask), (column_mask_hbm, column_mask), (row_mask_hbm, row_mask),
        ))
    ]
    for load in loads:
        load.start()

    def y_peer(step):
        return chan, lax.rem(y + step, Y) * ring + inner

    def z_peer(step):
        there = lax.rem(z + step, ZH * ZL)
        return x * ZH + there // ZL, y * ring + lax.rem(there, ZL) * CORES + core

    def x_peer(step):
        there = lax.rem(x * CORES + core + step, X * CORES)
        return there // CORES * ZH + z_hi, y * ring + z_lo * CORES + lax.rem(there, CORES)

    barrier = pltpu.get_barrier_semaphore()

    @pl.loop(1, seqs)
    def _(step):
        pl.semaphore_signal(barrier, inc=1, device_id=(chan, lax.rem(me + step, seqs)), device_id_type=MESH)

    greeted = seqs - 1
    for away in range(ZL):
        if ZH == 2:
            pl.semaphore_signal(
                barrier, inc=1,
                device_id=(x * ZH + 1 - z_hi, y * ring + away * CORES + core), device_id_type=MESH,
            )
            greeted += 1
    for step in range(1, X):
        for other in range(CORES):
            there = lax.rem(x + step, X) * ZH + z_hi
            pl.semaphore_signal(
                barrier, inc=1, device_id=(there, y * ring + z_lo * CORES + other), device_id_type=MESH
            )
            greeted += 1

    pick = onehot((seqs, width), same, lambda c: c // 2).astype(BF16)
    even = jnp.where(iota((1, width), 1) % 2 == 0, 1.0, 0.0).astype(BF16)
    odd = jnp.where(iota((1, width), 1) % 2 == 1, 1.0, 0.0).astype(BF16)

    def flip(read, i):
        def body(block, carry):
            value = read(pl.ds(pl.multiple_of(block * INNER, INNER), INNER))
            both = jnp.concatenate([value * even, value * odd], axis=0)
            flipped[pl.ds(pl.multiple_of(block * seqs, seqs), seqs), :] = dot(pick, both, (1, 1))
            return carry

        lax.fori_loop(i * MIDDLE, (i + 1) * MIDDLE, body, 0, unroll=8)

    def column_rows(i, start, count, d):
        return flipped[pl.ds((i * MIDDLE + start) * seqs + d, count, stride=seqs), :]

    def send(pack, buffer, target, start, count, slot):
        rows = pl.ds(start, count)

        def body(turn, carry):
            for place, away in enumerate(Y_ORDER):
                if away >= Y:
                    continue
                step = lax.rem(turn + place + 1, ring)
                to = lax.rem(y + away, Y) * ring + lax.rem(inner + step, ring)
                buffer[to, start : start + count, :] = pack(to).astype(BF16)

                def go():
                    pltpu.make_async_remote_copy(
                        src_ref=buffer.at[to, rows], dst_ref=target.at[me, rows],
                        send_sem=send_sem.at[slot], recv_sem=recv_sem.at[slot],
                        device_id=(chan, to), device_id_type=MESH,
                    ).start()

                if away == 0:
                    pl.when(step != 0)(go)
                else:
                    go()
            return carry

        lax.fori_loop(0, ring, body, 0)
        own = pltpu.make_async_copy(buffer.at[me, rows], target.at[me, rows], self_sem.at[slot])
        own.start()
        return own

    owns = []
    loads[0].wait()
    for i in range(2):
        flip(lambda rows: signal[rows, :], i)
        if i == 0:
            pl.semaphore_wait(barrier, greeted)
        owns.append(
            send(lambda d: column_rows(i, 0, MIDDLE, d), send_x, got_x, i * MIDDLE, MIDDLE, i)
        )

    loads[1].wait()
    for i in range(2):
        flip(lambda rows: (cotangent[rows, :].astype(F32) * signal[rows, :].astype(F32)).astype(BF16), i)
    for part, (start, count) in enumerate(zip(starts, PARTS)):
        def pack_part(d):
            return jnp.concatenate([column_rows(i, start, count, d) for i in range(2)], axis=0)

        owns.append(send(pack_part, send_g, got_g, 2 * start, 2 * count, 2 + part))

    for load in loads[2:]:
        load.wait()
    keep_row = spread_mask(row_mask[...], outer)
    keep_column = spread_mask(column_mask[...], MIDDLE)
    keep_depth = spread_mask(depth_mask[...], INNER)
    w_row = (row_ref[...].astype(F32) * keep_row).astype(BF16)
    w_row_t[...] = dot(onehot((outer, outer), same, same).astype(BF16), w_row, (1, 1)).astype(BF16)
    w_depth2[...] = twice((depth_ref[...].astype(F32) * keep_depth).astype(BF16))
    w_column2[...] = twice((column_ref[...].astype(F32) * keep_column).astype(BF16))

    def arrived(buffer, start, count, slot):
        owns[slot].wait()
        others = buffer.at[pl.ds(0, seqs - 1), pl.ds(start, count)]
        pltpu.make_async_copy(others, others, recv_sem.at[slot]).wait()

    for i in range(2):
        arrived(got_x, i * MIDDLE, MIDDLE, i)

    def signal_side(s, carry):
        field = got_x[s]
        one = dot(field, w_depth2[...], (1, 1)).astype(BF16)
        first[s] = one
        two = dot(w_column2[...], jnp.concatenate([field, one], axis=1), (1, 0))
        for start, count in zip(starts, PARTS):
            mixed[s, 2 * start : 2 * (start + count), :] = jnp.concatenate(
                [two[i * MIDDLE + start : i * MIDDLE + start + count, :LANES] for i in range(2)], axis=0
            ).astype(BF16)
        wide[pl.ds(pl.multiple_of(s * 2 * MIDDLE, 2 * MIDDLE), 2 * MIDDLE), :] = two[:, LANES:]
        return carry

    lax.fori_loop(0, seqs, signal_side, 0, unroll=4)

    def by_column(j, carry):
        second[j] = wide[pl.ds(j, outer, stride=MIDDLE), :].astype(BF16)
        return carry

    lax.fori_loop(0, MIDDLE, by_column, 0, unroll=4)

    grad_row = jnp.zeros((outer, outer), F32)
    grad_depth = jnp.zeros((LANES, LANES), F32)
    group = min(4, seqs)
    for part, (start, count) in enumerate(zip(starts, PARTS)):
        pair = 2 * count
        arrived(got_g, 2 * start, pair, 2 + part)

        def widen(s, carry):
            wide[pl.ds(pl.multiple_of(s * pair, pair), pair), :] = got_g[s, 2 * start : 2 * start + pair, :].astype(F32)
            return carry

        lax.fori_loop(0, seqs, widen, 0, unroll=8)

        def row_side(j, total):
            gated = wide[pl.ds(j, outer, stride=count), :].astype(BF16)
            back[pl.ds(j, outer, stride=count), :] = dot(w_row_t[...], gated, (1, 0))
            return total + dot(gated, second[start + j], (1, 1))

        grad_row = lax.fori_loop(0, count, row_side, grad_row, unroll=4)

        def back_side(block, carry):
            column, depth = carry
            rows = group * pair
            value = back[pl.ds(pl.multiple_of(block * rows, rows), rows), :]
            fields = mixed[pl.ds(block * group, group), 2 * start : 2 * start + pair, :].reshape(rows, LANES)
            depth = depth + dot(value.astype(BF16), fields, (0, 0))
            ours, theirs = [], []
            for s in range(group):
                at = s * pair
                ours.append(jnp.concatenate([value[at : at + count], value[at + count : at + pair]], axis=1))
                one = first[block * group + s]
                theirs.append(jnp.concatenate([one[:MIDDLE], one[MIDDLE:]], axis=1))
            ours = jnp.concatenate(ours, axis=0).astype(BF16)
            column = column + dot(ours, jnp.concatenate(theirs, axis=0), (1, 1))
            return column, depth

        column, grad_depth = lax.fori_loop(
            0, seqs // group, back_side,
            (jnp.zeros((group * count, group * MIDDLE), F32), grad_depth), unroll=2,
        )
        piece = jnp.zeros((count, MIDDLE), F32)
        for s in range(group):
            piece = piece + column[s * count : (s + 1) * count, s * MIDDLE : (s + 1) * MIDDLE]
        sums[outer + start : outer + start + count, :MIDDLE] = piece
    sums[:outer, :outer] = grad_row
    sums[outer:, MIDDLE:] = grad_depth[:INNER, :INNER] + grad_depth[INNER:, INNER:]

    def exchange(phase, count, peer, source, target):
        for step in FAR_FIRST:
            if step < count:
                to = peer(step)
                pltpu.make_async_remote_copy(
                    src_ref=source(to), dst_ref=target,
                    send_sem=part_send.at[phase], recv_sem=part_recv.at[phase],
                    device_id=to, device_id_type=MESH,
                ).start()

    def landed(phase, land, count):
        others = land.at[pl.ds(0, count - 1)]
        pltpu.make_async_copy(others, others, part_recv.at[phase]).wait()

    def added(land):
        total = land[0]
        for slot in range(1, land.shape[0]):
            total = total + land[slot]
        return total

    def rows_of(place):
        return pl.ds(pl.multiple_of(place * local_rows, 8), local_rows)

    def place_of(to):
        return to[0] // ZH * CORES + to[1] % CORES

    place = x * CORES + core
    land_1[place] = sums[rows_of(place), :]
    exchange(0, X * CORES, x_peer, lambda to: sums.at[rows_of(place_of(to))], land_1.at[place])
    landed(0, land_1, X * CORES)
    sum_1[...] = added(land_1)
    land_2[z] = sum_1[...]
    exchange(1, ZH * ZL, z_peer, lambda to: sum_1, land_2.at[z])
    landed(1, land_2, ZH * ZL)
    sum_2[...] = added(land_2)
    land_3[y] = sum_2[...]
    exchange(2, Y, y_peer, lambda to: sum_2, land_3.at[y])
    landed(2, land_3, Y)
    sum_3[...] = added(land_3)
    land_4[place] = sum_3[...]
    exchange(3, X * CORES, x_peer, lambda to: sum_3, land_4.at[place])
    landed(3, land_4, X * CORES)

    whole = land_4[...].reshape(outer + MIDDLE, LANES)
    inner_count = 1.0 / math.sqrt(SEQLEN * CHANNELS // MIDDLE)
    outer_count = 1.0 / math.sqrt(SEQLEN * CHANNELS // outer)
    out_row[...] = jnp.where(keep_row > 0.5, whole[:outer, :outer] * outer_count, 0.0)
    out_column[...] = jnp.where(keep_column > 0.5, whole[outer:, :MIDDLE] * inner_count, 0.0)
    out_depth[...] = jnp.where(keep_depth > 0.5, whole[outer:, MIDDLE:] * inner_count, 0.0)

    def sent(buffer, start, count, slot):
        others = buffer.at[pl.ds(0, seqs - 1), pl.ds(start, count)]
        pltpu.make_async_copy(others, others, send_sem.at[slot]).wait()

    for i in range(2):
        sent(send_x, i * MIDDLE, MIDDLE, i)
    for part, (start, count) in enumerate(zip(starts, PARTS)):
        sent(send_g, 2 * start, 2 * count, 2 + part)
    for phase, (land, count) in enumerate(
        ((land_1, X * CORES), (land_2, ZH * ZL), (land_3, Y), (land_4, X * CORES))
    ):
        others = land.at[pl.ds(0, count - 1)]
        pltpu.make_async_copy(others, others, part_send.at[phase]).wait()


def per_device(
    signal, cotangent, depth_factor, column_factor, row_factor, depth_mask, column_mask, row_mask
):
    seqs = Y * ZL * CORES
    outer = row_factor.shape[0]
    rows, width = signal.shape
    local_rows = (outer + MIDDLE) // (X * CORES)
    vmem = pl.BlockSpec(memory_space=pltpu.VMEM)
    hbm = pl.BlockSpec(memory_space=pltpu.HBM)
    return pl.pallas_call(
        functools.partial(kernel, seqs, outer),
        out_shape=(
            jax.ShapeDtypeStruct((INNER, INNER), F32),
            jax.ShapeDtypeStruct((MIDDLE, MIDDLE), F32),
            jax.ShapeDtypeStruct((outer, outer), F32),
        ),
        in_specs=[hbm] * 8,
        out_specs=(vmem, vmem, vmem),
        scratch_shapes=[
            pltpu.VMEM((rows, width), BF16),
            pltpu.VMEM((rows, width), BF16),
        ] + [
            pltpu.VMEM(a.shape, a.dtype)
            for a in (depth_factor, column_factor, row_factor, depth_mask, column_mask, row_mask)
        ] + [
            pltpu.VMEM((2 * MIDDLE * seqs, LANES), F32),
            pltpu.VMEM((seqs, 2 * MIDDLE, LANES), BF16),
            pltpu.VMEM((seqs, 2 * MIDDLE, LANES), BF16),
            pltpu.VMEM((seqs, 2 * MIDDLE, LANES), BF16),
            pltpu.VMEM((seqs, 2 * MIDDLE, LANES), BF16),
            pltpu.VMEM((seqs, 2 * MIDDLE, LANES), BF16),
            pltpu.VMEM((seqs, 2 * MIDDLE, LANES), BF16),
            pltpu.VMEM((MIDDLE, outer, LANES), BF16),
            pltpu.VMEM((outer * MIDDLE, LANES), F32),
            pltpu.VMEM((outer * max(PARTS), LANES), F32),
            pltpu.VMEM((outer, outer), BF16),
            pltpu.VMEM((LANES, LANES), BF16),
            pltpu.VMEM((LANES, LANES), BF16),
            pltpu.VMEM((outer + MIDDLE, LANES), F32),
            pltpu.VMEM((X * CORES, local_rows, LANES), F32),
            pltpu.VMEM((ZH * ZL, local_rows, LANES), F32),
            pltpu.VMEM((Y, local_rows, LANES), F32),
            pltpu.VMEM((X * CORES, local_rows, LANES), F32),
            pltpu.VMEM((local_rows, LANES), F32),
            pltpu.VMEM((local_rows, LANES), F32),
            pltpu.VMEM((local_rows, LANES), F32),
            pltpu.SemaphoreType.DMA((8,)),
            pltpu.SemaphoreType.DMA((2 + len(PARTS),)),
            pltpu.SemaphoreType.DMA((2 + len(PARTS),)),
            pltpu.SemaphoreType.DMA((2 + len(PARTS),)),
            pltpu.SemaphoreType.DMA((4,)),
            pltpu.SemaphoreType.DMA((4,)),
        ],
        compiler_params=pltpu.CompilerParams(
            collective_id=0, has_side_effects=True, vmem_limit_bytes=60 * 2**20
        ),
        cost_estimate=pl.CostEstimate(flops=1_300_000_000, bytes_accessed=4 * 2**20, transcendentals=0),
    )(signal, cotangent, depth_factor, column_factor, row_factor, depth_mask, column_mask, row_mask)


def solution(mesh):
    in_specs = (P("seq", "chan"), P("seq", "chan"), P(), P(), P(), P(), P(), P())
    out_specs = (P(), P(), P())
    return jax.shard_map(
        per_device, mesh=mesh, in_specs=in_specs, out_specs=out_specs, check_vma=False
    )
```

time: 149 us -> 144 us (0.966)
  local copies, waits for them, and re-layouts: 9.27 us -> 4.22 us
    unnamed x19 -> x3, local copies, waits for them, and re-layouts: 9.27 us -> 4.22 us
where the time goes in v2:
time: 144 us
  Pallas kernels  139 us (97%)
  local copies, waits for them, and re-layouts  4.22 us (3%)
    pallas_call x1, Pallas kernels, per_device(): pl.pallas_call(functools.partial(kernel, seqs, outer), out_shape=(jax.Sha...  139 us
    unnamed x3, local copies, waits for them, and re-layouts  4.22 us

profile of v2, /device:TPU:1, one launch (start us, length us, event | category | flops | bytes accessed | tf_op | source)
XLA Modules:
  0.0 143.8 jit_solution(14962898011501902369)
XLA Ops:
  0.6 138.9 %shard_map.103 = (f32[64,64]{1,0:T(8,128)}, f32[64,64]{1,0:T(8,128)}, f32[128,128]{1,0:T(8,128)}) custom-call(bf16[8192,128]{1,0:T(8,128)(2,1)} %signal_hbm.1, bf16[8192,128]{1,0:T(8,128)(2,1)} %cotangent_hbm.1, bf16[64,64]{1,0:T(8,128)(2,1)} %depth_hbm.1, bf16[64,64]{1,0:T(8,128)(2,1)} %column_hbm.1, bf16[128,128]{1,0:T(8,128)(2,1)} %row_hbm.1, ...), custom_call_target="tpu_custom_call" | custom-call | flops 1300000000 | bytes 4194304 | tf_op jit(solution)/shard_map/pallas_call | solution.py:343
  139.6 1.4 copy.14
  140.9 1.4 copy.15
  142.3 1.5 %copy.16 = f32[128,128]{1,0:T(8,128)} copy(f32[128,128]{1,0:T(8,128)} %get-tuple-element.8) | data formatting | bytes 131072

commit v3 on v2

--- a/solution.py
+++ b/solution.py
@@ -15,6 +15,7 @@
 LANES = 128
 X, ZH, Y, ZL, CORES = 4, 2, 8, 4, 2
 PARTS = (16, 16, 16, 8, 8)
+HEAD = ((0, 0, 16), (0, 16, 48), (1, 0, 64))
 Y_ORDER = (1, 7, 2, 6, 3, 5, 4, 0)
 FAR_FIRST = (4, 3, 5, 2, 6, 1, 7)
 F32, BF16 = jnp.float32, jnp.bfloat16
@@ -59,7 +60,7 @@
     signal_hbm, cotangent_hbm, depth_hbm, column_hbm, row_hbm, depth_mask_hbm, column_mask_hbm, row_mask_hbm,
     out_depth, out_column, out_row,
     signal, cotangent, depth_ref, column_ref, row_ref, depth_mask, column_mask, row_mask,
-    flipped, send_x, send_g, got_x, got_g, first, mixed, second, wide, back,
+    flipped, send_x, send_g, got_x, got_g, first_t, mixed_t, second, wide, tall, back,
     w_row_t, w_depth2, w_column2, sums, land_1, land_2, land_3, land_4, sum_1, sum_2, sum_3,
     load_sem, self_sem, send_sem, recv_sem, part_send, part_recv,
 ):
@@ -121,14 +122,19 @@
     even = jnp.where(iota((1, width), 1) % 2 == 0, 1.0, 0.0).astype(BF16)
     odd = jnp.where(iota((1, width), 1) % 2 == 1, 1.0, 0.0).astype(BF16)
 
-    def flip(read, i):
+    def flip(read, i, start, count):
         def body(block, carry):
-            value = read(pl.ds(pl.multiple_of(block * INNER, INNER), INNER))
-            both = jnp.concatenate([value * even, value * odd], axis=0)
-            flipped[pl.ds(pl.multiple_of(block * seqs, seqs), seqs), :] = dot(pick, both, (1, 1))
+            value = read(pl.ds(pl.multiple_of(block * 2 * INNER, 2 * INNER), 2 * INNER))
+            ones, twos = value * even, value * odd
+            both = [ones[:INNER], twos[:INNER], ones[INNER:], twos[INNER:]]
+            turned = dot(pick, jnp.concatenate(both, axis=0), (1, 1))
+            at = pl.multiple_of(block * 2 * seqs, 2 * seqs)
+            flipped[pl.ds(at, seqs), :] = turned[:, :LANES]
+            flipped[pl.ds(at + seqs, seqs), :] = turned[:, LANES:]
             return carry
 
-        lax.fori_loop(i * MIDDLE, (i + 1) * MIDDLE, body, 0, unroll=8)
+        at = (i * MIDDLE + start) // 2
+        lax.fori_loop(at, at + count // 2, body, 0, unroll=8)
 
     def column_rows(i, start, count, d):
         return flipped[pl.ds((i * MIDDLE + start) * seqs + d, count, stride=seqs), :]
@@ -164,22 +170,25 @@
 
     owns = []
     loads[0].wait()
-    for i in range(2):
-        flip(lambda rows: signal[rows, :], i)
-        if i == 0:
+    for part, (i, start, count) in enumerate(HEAD):
+        flip(lambda rows: signal[rows, :], i, start, count)
+        if part == 0:
             pl.semaphore_wait(barrier, greeted)
-        owns.append(
-            send(lambda d: column_rows(i, 0, MIDDLE, d), send_x, got_x, i * MIDDLE, MIDDLE, i)
-        )
+        owns.append(send(
+            lambda d: column_rows(i, start, count, d), send_x, got_x, i * MIDDLE + start, count, part
+        ))
 
     loads[1].wait()
     for i in range(2):
-        flip(lambda rows: (cotangent[rows, :].astype(F32) * signal[rows, :].astype(F32)).astype(BF16), i)
+        flip(
+            lambda rows: (cotangent[rows, :].astype(F32) * signal[rows, :].astype(F32)).astype(BF16),
+            i, 0, MIDDLE,
+        )
     for part, (start, count) in enumerate(zip(starts, PARTS)):
         def pack_part(d):
             return jnp.concatenate([column_rows(i, start, count, d) for i in range(2)], axis=0)
 
-        owns.append(send(pack_part, send_g, got_g, 2 * start, 2 * count, 2 + part))
+        owns.append(send(pack_part, send_g, got_g, 2 * start, 2 * count, len(HEAD) + part))
 
     for load in loads[2:]:
         load.wait()
@@ -196,75 +205,72 @@
         others = buffer.at[pl.ds(0, seqs - 1), pl.ds(start, count)]
         pltpu.make_async_copy(others, others, recv_sem.at[slot]).wait()
 
-    for i in range(2):
-        arrived(got_x, i * MIDDLE, MIDDLE, i)
+    for part, (i, start, count) in enumerate(HEAD):
+        arrived(got_x, i * MIDDLE + start, count, part)
 
     def signal_side(s, carry):
         field = got_x[s]
-        one = dot(field, w_depth2[...], (1, 1)).astype(BF16)
-        first[s] = one
-        two = dot(w_column2[...], jnp.concatenate([field, one], axis=1), (1, 0))
-        for start, count in zip(starts, PARTS):
-            mixed[s, 2 * start : 2 * (start + count), :] = jnp.concatenate(
-                [two[i * MIDDLE + start : i * MIDDLE + start + count, :LANES] for i in range(2)], axis=0
-            ).astype(BF16)
-        wide[pl.ds(pl.multiple_of(s * 2 * MIDDLE, 2 * MIDDLE), 2 * MIDDLE), :] = two[:, LANES:]
+        first = dot(field, w_depth2[...], (1, 1)).astype(BF16)
+        first_t[pl.ds(pl.multiple_of(s * LANES, LANES), LANES), :] = dot(w_depth2[...], field, (1, 1)).astype(BF16)
+        both = dot(w_column2[...], jnp.concatenate([field, first], axis=1), (1, 0))
+        rows = pl.ds(pl.multiple_of(s * 2 * MIDDLE, 2 * MIDDLE), 2 * MIDDLE)
+        tall[rows, :] = both[:, :LANES]
+        wide[rows, :] = both[:, LANES:]
         return carry
 
     lax.fori_loop(0, seqs, signal_side, 0, unroll=4)
 
-    def by_column(j, carry):
-        second[j] = wide[pl.ds(j, outer, stride=MIDDLE), :].astype(BF16)
+    same_lane = onehot((LANES, LANES), same, same).astype(BF16)
+
+    def by_column(two, carry):
+        at = [pl.ds(2 * two + j, outer, stride=MIDDLE) for j in range(2)]
+        second[two] = jnp.concatenate([wide[rows, :] for rows in at], axis=1).astype(BF16)
+        mixed = jnp.concatenate([tall[rows, :] for rows in at], axis=0).astype(BF16)
+        mixed_t[two] = dot(same_lane, mixed, (1, 1)).astype(BF16)
         return carry
 
-    lax.fori_loop(0, MIDDLE, by_column, 0, unroll=4)
+    lax.fori_loop(0, MIDDLE // 2, by_column, 0, unroll=4)
 
     grad_row = jnp.zeros((outer, outer), F32)
-    grad_depth = jnp.zeros((LANES, LANES), F32)
-    group = min(4, seqs)
+    grad_depth_t = jnp.zeros((LANES, LANES), F32)
     for part, (start, count) in enumerate(zip(starts, PARTS)):
         pair = 2 * count
-        arrived(got_g, 2 * start, pair, 2 + part)
+        arrived(got_g, 2 * start, pair, len(HEAD) + part)
 
         def widen(s, carry):
             wide[pl.ds(pl.multiple_of(s * pair, pair), pair), :] = got_g[s, 2 * start : 2 * start + pair, :].astype(F32)
             return carry
 
-        lax.fori_loop(0, seqs, widen, 0, unroll=8)
-
-        def row_side(j, total):
-            gated = wide[pl.ds(j, outer, stride=count), :].astype(BF16)
-            back[pl.ds(j, outer, stride=count), :] = dot(w_row_t[...], gated, (1, 0))
-            return total + dot(gated, second[start + j], (1, 1))
-
-        grad_row = lax.fori_loop(0, count, row_side, grad_row, unroll=4)
-
-        def back_side(block, carry):
-            column, depth = carry
-            rows = group * pair
-            value = back[pl.ds(pl.multiple_of(block * rows, rows), rows), :]
-            fields = mixed[pl.ds(block * group, group), 2 * start : 2 * start + pair, :].reshape(rows, LANES)
-            depth = depth + dot(value.astype(BF16), fields, (0, 0))
-            ours, theirs = [], []
-            for s in range(group):
-                at = s * pair
-                ours.append(jnp.concatenate([value[at : at + count], value[at + count : at + pair]], axis=1))
-                one = first[block * group + s]
-                theirs.append(jnp.concatenate([one[:MIDDLE], one[MIDDLE:]], axis=1))
-            ours = jnp.concatenate(ours, axis=0).astype(BF16)
-            column = column + dot(ours, jnp.concatenate(theirs, axis=0), (1, 1))
-            return column, depth
-
-        column, grad_depth = lax.fori_loop(
-            0, seqs // group, back_side,
-            (jnp.zeros((group * count, group * MIDDLE), F32), grad_depth), unroll=2,
+        lax.fori_loop(0, seqs, widen, 0, unroll=16 if seqs % 16 == 0 else 1)
+
+        def column_side(two, carry):
+            row, depth_t = carry
+            at = [pl.ds(2 * two + j, outer, stride=count) for j in range(2)]
+            gated = jnp.concatenate([wide[rows, :] for rows in at], axis=1).astype(BF16)
+            value = dot(w_row_t[...], gated, (1, 0))
+            for j in range(2):
+                back[at[j], :] = value[:, j * LANES : (j + 1) * LANES]
+            value = value.astype(BF16)
+            value = jnp.concatenate([value[:, :LANES], value[:, LANES:]], axis=0)
+            row = row + dot(gated, second[start // 2 + two], (1, 1))
+            depth_t = depth_t + dot(mixed_t[start // 2 + two], value, (1, 0))
+            return row, depth_t
+
+        grad_row, grad_depth_t = lax.fori_loop(
+            0, count // 2, column_side, (grad_row, grad_depth_t), unroll=2
         )
-        piece = jnp.zeros((count, MIDDLE), F32)
-        for s in range(group):
-            piece = piece + column[s * count : (s + 1) * count, s * MIDDLE : (s + 1) * MIDDLE]
-        sums[outer + start : outer + start + count, :MIDDLE] = piece
+
+        def back_side(two, column):
+            rows = [pl.ds(pl.multiple_of((2 * two + s) * pair, pair), pair) for s in range(2)]
+            value = jnp.concatenate([back[at, :] for at in rows], axis=1).astype(BF16)
+            return column + dot(value, first_t[pl.ds(pl.multiple_of(two * 2 * LANES, 2 * LANES), 2 * LANES), :], (1, 0))
+
+        column = lax.fori_loop(
+            0, seqs // 2, back_side, jnp.zeros((pair, LANES), F32), unroll=min(8, seqs // 4)
+        )
+        sums[outer + start : outer + start + count, :MIDDLE] = column[:count, :MIDDLE] + column[count:, MIDDLE:]
     sums[:outer, :outer] = grad_row
-    sums[outer:, MIDDLE:] = grad_depth[:INNER, :INNER] + grad_depth[INNER:, INNER:]
+    sums[outer:, MIDDLE:] = grad_depth_t[:INNER, :INNER] + grad_depth_t[INNER:, INNER:]
 
     def exchange(phase, count, peer, source, target):
         for step in FAR_FIRST:
@@ -314,21 +320,33 @@
     outer_count = 1.0 / math.sqrt(SEQLEN * CHANNELS // outer)
     out_row[...] = jnp.where(keep_row > 0.5, whole[:outer, :outer] * outer_count, 0.0)
     out_column[...] = jnp.where(keep_column > 0.5, whole[outer:, :MIDDLE] * inner_count, 0.0)
-    out_depth[...] = jnp.where(keep_depth > 0.5, whole[outer:, MIDDLE:] * inner_count, 0.0)
+    out_depth[...] = jnp.where(keep_depth > 0.5, whole[outer:, MIDDLE:].T * inner_count, 0.0)
 
     def sent(buffer, start, count, slot):
         others = buffer.at[pl.ds(0, seqs - 1), pl.ds(start, count)]
         pltpu.make_async_copy(others, others, send_sem.at[slot]).wait()
 
-    for i in range(2):
-        sent(send_x, i * MIDDLE, MIDDLE, i)
+    for part, (i, start, count) in enumerate(HEAD):
+        sent(send_x, i * MIDDLE + start, count, part)
     for part, (start, count) in enumerate(zip(starts, PARTS)):
-        sent(send_g, 2 * start, 2 * count, 2 + part)
+        sent(send_g, 2 * start, 2 * count, len(HEAD) + part)
     for phase, (land, count) in enumerate(
         ((land_1, X * CORES), (land_2, ZH * ZL), (land_3, Y), (land_4, X * CORES))
     ):
         others = land.at[pl.ds(0, count - 1)]
         pltpu.make_async_copy(others, others, part_send.at[phase]).wait()
+
+
+def hand_over(*refs):
+    sources, targets, sem = refs[:3], refs[3:6], refs[6]
+    copies = [
+        pltpu.make_async_copy(source, target, sem.at[place])
+        for place, (source, target) in enumerate(zip(sources, targets))
+    ]
+    for copy in copies:
+        copy.start()
+    for copy in copies:
+        copy.wait()
 
 
 def per_device(
@@ -340,13 +358,14 @@
     local_rows = (outer + MIDDLE) // (X * CORES)
     vmem = pl.BlockSpec(memory_space=pltpu.VMEM)
     hbm = pl.BlockSpec(memory_space=pltpu.HBM)
-    return pl.pallas_call(
+    shapes = (
+        jax.ShapeDtypeStruct((INNER, INNER), F32),
+        jax.ShapeDtypeStruct((MIDDLE, MIDDLE), F32),
+        jax.ShapeDtypeStruct((outer, outer), F32),
+    )
+    results = pl.pallas_call(
         functools.partial(kernel, seqs, outer),
-        out_shape=(
-            jax.ShapeDtypeStruct((INNER, INNER), F32),
-            jax.ShapeDtypeStruct((MIDDLE, MIDDLE), F32),
-            jax.ShapeDtypeStruct((outer, outer), F32),
-        ),
+        out_shape=shapes,
         in_specs=[hbm] * 8,
         out_specs=(vmem, vmem, vmem),
         scratch_shapes=[
@@ -361,9 +380,10 @@
             pltpu.VMEM((seqs, 2 * MIDDLE, LANES), BF16),
             pltpu.VMEM((seqs, 2 * MIDDLE, LANES), BF16),
             pltpu.VMEM((seqs, 2 * MIDDLE, LANES), BF16),
-            pltpu.VMEM((seqs, 2 * MIDDLE, LANES), BF16),
-            pltpu.VMEM((seqs, 2 * MIDDLE, LANES), BF16),
-            pltpu.VMEM((MIDDLE, outer, LANES), BF16),
+            pltpu.VMEM((seqs * LANES, 2 * MIDDLE), BF16),
+            pltpu.VMEM((MIDDLE // 2, LANES, 2 * outer), BF16),
+            pltpu.VMEM((MIDDLE // 2, outer, 2 * LANES), BF16),
+            pltpu.VMEM((outer * MIDDLE, LANES), F32),
             pltpu.VMEM((outer * MIDDLE, LANES), F32),
             pltpu.VMEM((outer * max(PARTS), LANES), F32),
             pltpu.VMEM((outer, outer), BF16),
@@ -378,9 +398,9 @@
             pltpu.VMEM((local_rows, LANES), F32),
             pltpu.VMEM((local_rows, LANES), F32),
             pltpu.SemaphoreType.DMA((8,)),
-            pltpu.SemaphoreType.DMA((2 + len(PARTS),)),
-            pltpu.SemaphoreType.DMA((2 + len(PARTS),)),
-            pltpu.SemaphoreType.DMA((2 + len(PARTS),)),
+            pltpu.SemaphoreType.DMA((len(HEAD) + len(PARTS),)),
+            pltpu.SemaphoreType.DMA((len(HEAD) + len(PARTS),)),
+            pltpu.SemaphoreType.DMA((len(HEAD) + len(PARTS),)),
             pltpu.SemaphoreType.DMA((4,)),
             pltpu.SemaphoreType.DMA((4,)),
         ],
@@ -389,6 +409,14 @@
         ),
         cost_estimate=pl.CostEstimate(flops=1_300_000_000, bytes_accessed=4 * 2**20, transcendentals=0),
     )(signal, cotangent, depth_factor, column_factor, row_factor, depth_mask, column_mask, row_mask)
+    return pl.pallas_call(
+        hand_over,
+        out_shape=shapes,
+        in_specs=[hbm] * 3,
+        out_specs=(hbm, hbm, hbm),
+        scratch_shapes=[pltpu.SemaphoreType.DMA((3,))],
+        compiler_params=pltpu.CompilerParams(vmem_limit_bytes=60 * 2**20),
+    )(*results)
 
 
 def solution(mesh):

time: 144 us -> 138 us (0.958)
  local copies, waits for them, and re-layouts: 4.22 us -> 0 us
  Pallas kernels: 139 us -> 137 us
    unnamed x3 -> x0, local copies, waits for them, and re-layouts: 4.22 us -> none
    pallas_call x1 -> x2, Pallas kernels: 139 us -> 137 us  [the longest x1 132 us: per_device(): pl.pallas_call(functools.partial(kernel, seqs, outer), out_shape=shapes,...]
where the time goes in v3:
time: 138 us; the launch traced here: 137 us
  Pallas kernels  137 us (99%)
    pallas_call x1, Pallas kernels, per_device(): pl.pallas_call(functools.partial(kernel, seqs, outer), out_shape=shapes,...  132 us
    pallas_call x1, Pallas kernels, per_device(): pl.pallas_call(hand_over, out_shape=shapes, in_specs=[hbm] * 3, out_specs...  5.1 us

profile of v3, /device:TPU:1, one launch (start us, length us, event | category | flops | bytes accessed | tf_op | source)
XLA Modules:
  0.0 137.5 jit_solution(15720221586216628291)
XLA Ops:
  0.6 131.7 %shard_map.103 = (f32[64,64]{1,0:T(8,128)}, f32[64,64]{1,0:T(8,128)}, f32[128,128]{1,0:T(8,128)}) custom-call(bf16[8192,128]{1,0:T(8,128)(2,1)} %signal_hbm.1, bf16[8192,128]{1,0:T(8,128)(2,1)} %cotangent_hbm.1, bf16[64,64]{1,0:T(8,128)(2,1)} %depth_hbm.1, bf16[64,64]{1,0:T(8,128)(2,1)} %column_hbm.1, bf16[128,128]{1,0:T(8,128)(2,1)} %row_hbm.1, ...), custom_call_target="tpu_custom_call" | custom-call | flops 1300000000 | bytes 4194304 | tf_op jit(solution)/shard_map/pallas_call | solution.py:366
  132.4 5.1 %shard_map.104 = (f32[64,64]{1,0:T(8,128)}, f32[64,64]{1,0:T(8,128)}, f32[128,128]{1,0:T(8,128)}) custom-call(f32[64,64]{1,0:T(8,128)} %get-tuple-element.6.refs_0_, f32[64,64]{1,0:T(8,128)} %get-tuple-element.7.refs_1_, f32[128,128]{1,0:T(8,128)} %get-tuple-element.8.refs_2_), custom_call_target="tpu_custom_call" | custom-call | tf_op jit(solution)/shard_map/pallas_call | solution.py:412

commit v4 on v3

--- a/solution.py
+++ b/solution.py
@@ -98,8 +98,9 @@
 
     barrier = pltpu.get_barrier_semaphore()
 
-    @pl.loop(1, seqs)
-    def _(step):
+    @pl.loop(0, seqs - 1)
+    def _(turn):
+        step = 1 + lax.rem(turn + seqs // 2 - ring // 2, seqs - 1)
         pl.semaphore_signal(barrier, inc=1, device_id=(chan, lax.rem(me + step, seqs)), device_id_type=MESH)
 
     greeted = seqs - 1
@@ -338,15 +339,22 @@
 
 
 def hand_over(*refs):
-    sources, targets, sem = refs[:3], refs[3:6], refs[6]
-    copies = [
-        pltpu.make_async_copy(source, target, sem.at[place])
-        for place, (source, target) in enumerate(zip(sources, targets))
+    sources, targets, held, sem = refs[:3], refs[3:6], refs[6:9], refs[9]
+    loads = [
+        pltpu.make_async_copy(source, place, sem.at[i])
+        for i, (source, place) in enumerate(zip(sources, held))
     ]
-    for copy in copies:
-        copy.start()
-    for copy in copies:
-        copy.wait()
+    stores = [
+        pltpu.make_async_copy(place, target, sem.at[3 + i])
+        for i, (place, target) in enumerate(zip(held, targets))
+    ]
+    for load in loads:
+        load.start()
+    for load, store in zip(loads, stores):
+        load.wait()
+        store.start()
+    for store in stores:
+        store.wait()
 
 
 def per_device(
@@ -414,7 +422,7 @@
         out_shape=shapes,
         in_specs=[hbm] * 3,
         out_specs=(hbm, hbm, hbm),
-        scratch_shapes=[pltpu.SemaphoreType.DMA((3,))],
+        scratch_shapes=[pltpu.VMEM(a.shape, a.dtype) for a in shapes] + [pltpu.SemaphoreType.DMA((6,))],
         compiler_params=pltpu.CompilerParams(vmem_limit_bytes=60 * 2**20),
     )(*results)
 

time: 138 us -> 135 us (0.978)
  Pallas kernels: 137 us -> 134 us
    pallas_call x1, Pallas kernels: 5.1 us -> 1.56 us  [per_device(): pl.pallas_call(hand_over, out_shape=shapes, in_specs=[hbm] * 3, out_specs...]
where the time goes in v4:
time: 135 us
  Pallas kernels  134 us (99%)
    pallas_call x1, Pallas kernels, per_device(): pl.pallas_call(functools.partial(kernel, seqs, outer), out_shape=shapes,...  133 us

profile of v4, /device:TPU:1, one launch (start us, length us, event | category | flops | bytes accessed | tf_op | source)
XLA Modules:
  0.0 134.8 jit_solution(9241747346605344597)
XLA Ops:
  0.6 132.6 %shard_map.103 = (f32[64,64]{1,0:T(8,128)}, f32[64,64]{1,0:T(8,128)}, f32[128,128]{1,0:T(8,128)}) custom-call(bf16[8192,128]{1,0:T(8,128)(2,1)} %signal_hbm.1, bf16[8192,128]{1,0:T(8,128)(2,1)} %cotangent_hbm.1, bf16[64,64]{1,0:T(8,128)(2,1)} %depth_hbm.1, bf16[64,64]{1,0:T(8,128)(2,1)} %column_hbm.1, bf16[128,128]{1,0:T(8,128)(2,1)} %row_hbm.1, ...), custom_call_target="tpu_custom_call" | custom-call | flops 1300000000 | bytes 4194304 | tf_op jit(solution)/shard_map/pallas_call | solution.py:374
  133.2 1.6 %shard_map.104 = (f32[64,64]{1,0:T(8,128)}, f32[64,64]{1,0:T(8,128)}, f32[128,128]{1,0:T(8,128)}) custom-call(f32[64,64]{1,0:T(8,128)} %get-tuple-element.6.refs_0_, f32[64,64]{1,0:T(8,128)} %get-tuple-element.7.refs_1_, f32[128,128]{1,0:T(8,128)} %get-tuple-element.8.refs_2_), custom_call_target="tpu_custom_call" | custom-call | tf_op jit(solution)/shard_map/pallas_call | solution.py:420

commit v5 on v4

--- a/solution.py
+++ b/solution.py
@@ -267,7 +267,7 @@
             return column + dot(value, first_t[pl.ds(pl.multiple_of(two * 2 * LANES, 2 * LANES), 2 * LANES), :], (1, 0))
 
         column = lax.fori_loop(
-            0, seqs // 2, back_side, jnp.zeros((pair, LANES), F32), unroll=min(8, seqs // 4)
+            0, seqs // 2, back_side, jnp.zeros((pair, LANES), F32), unroll=min(16, seqs // 4)
         )
         sums[outer + start : outer + start + count, :MIDDLE] = column[:count, :MIDDLE] + column[count:, MIDDLE:]
     sums[:outer, :outer] = grad_row
@@ -300,20 +300,20 @@
         return to[0] // ZH * CORES + to[1] % CORES
 
     place = x * CORES + core
+    exchange(0, X * CORES, x_peer, lambda to: sums.at[rows_of(place_of(to))], land_1.at[place])
     land_1[place] = sums[rows_of(place), :]
-    exchange(0, X * CORES, x_peer, lambda to: sums.at[rows_of(place_of(to))], land_1.at[place])
     landed(0, land_1, X * CORES)
     sum_1[...] = added(land_1)
+    exchange(1, ZH * ZL, z_peer, lambda to: sum_1, land_2.at[z])
     land_2[z] = sum_1[...]
-    exchange(1, ZH * ZL, z_peer, lambda to: sum_1, land_2.at[z])
     landed(1, land_2, ZH * ZL)
     sum_2[...] = added(land_2)
+    exchange(2, Y, y_peer, lambda to: sum_2, land_3.at[y])
     land_3[y] = sum_2[...]
-    exchange(2, Y, y_peer, lambda to: sum_2, land_3.at[y])
     landed(2, land_3, Y)
     sum_3[...] = added(land_3)
+    exchange(3, X * CORES, x_peer, lambda to: sum_3, land_4.at[place])
     land_4[place] = sum_3[...]
-    exchange(3, X * CORES, x_peer, lambda to: sum_3, land_4.at[place])
     landed(3, land_4, X * CORES)
 
     whole = land_4[...].reshape(outer + MIDDLE, LANES)
@@ -383,7 +383,7 @@
             pltpu.VMEM(a.shape, a.dtype)
             for a in (depth_factor, column_factor, row_factor, depth_mask, column_mask, row_mask)
         ] + [
-            pltpu.VMEM((2 * MIDDLE * seqs, LANES), F32),
+            pltpu.VMEM((2 * MIDDLE * seqs + seqs, LANES), F32),
             pltpu.VMEM((seqs, 2 * MIDDLE, LANES), BF16),
             pltpu.VMEM((seqs, 2 * MIDDLE, LANES), BF16),
             pltpu.VMEM((seqs, 2 * MIDDLE, LANES), BF16),
@@ -391,9 +391,9 @@
             pltpu.VMEM((seqs * LANES, 2 * MIDDLE), BF16),
             pltpu.VMEM((MIDDLE // 2, LANES, 2 * outer), BF16),
             pltpu.VMEM((MIDDLE // 2, outer, 2 * LANES), BF16),
-            pltpu.VMEM((outer * MIDDLE, LANES), F32),
-            pltpu.VMEM((outer * MIDDLE, LANES), F32),
-            pltpu.VMEM((outer * max(PARTS), LANES), F32),
+            pltpu.VMEM((outer * MIDDLE + MIDDLE, LANES), F32),
+            pltpu.VMEM((outer * MIDDLE + MIDDLE, LANES), F32),
+            pltpu.VMEM((outer * max(PARTS) + max(PARTS), LANES), F32),
             pltpu.VMEM((outer, outer), BF16),
             pltpu.VMEM((LANES, LANES), BF16),
             pltpu.VMEM((LANES, LANES), BF16),

time: 135 us -> 134 us (level)
  no operation moved by 1% of the time
where the time goes in v5:
time: 134 us
  Pallas kernels  134 us (100%)
    pallas_call x1, Pallas kernels, per_device(): pl.pallas_call(functools.partial(kernel, seqs, outer), out_shape=shapes,...  132 us

profile of v5, /device:TPU:1, one launch (start us, length us, event | category | flops | bytes accessed | tf_op | source)
XLA Modules:
  0.0 134.3 jit_solution(14586830912862880410)
XLA Ops:
  0.6 132.1 %shard_map.103 = (f32[64,64]{1,0:T(8,128)}, f32[64,64]{1,0:T(8,128)}, f32[128,128]{1,0:T(8,128)}) custom-call(bf16[8192,128]{1,0:T(8,128)(2,1)} %signal_hbm.1, bf16[8192,128]{1,0:T(8,128)(2,1)} %cotangent_hbm.1, bf16[64,64]{1,0:T(8,128)(2,1)} %depth_hbm.1, bf16[64,64]{1,0:T(8,128)(2,1)} %column_hbm.1, bf16[128,128]{1,0:T(8,128)(2,1)} %row_hbm.1, ...), custom_call_target="tpu_custom_call" | custom-call | flops 1300000000 | bytes 4194304 | tf_op jit(solution)/shard_map/pallas_call | solution.py:374
  132.7 1.6 %shard_map.104 = (f32[64,64]{1,0:T(8,128)}, f32[64,64]{1,0:T(8,128)}, f32[128,128]{1,0:T(8,128)}) custom-call(f32[64,64]{1,0:T(8,128)} %get-tuple-element.6.refs_0_, f32[64,64]{1,0:T(8,128)} %get-tuple-element.7.refs_1_, f32[128,128]{1,0:T(8,128)} %get-tuple-element.8.refs_2_), custom_call_target="tpu_custom_call" | custom-call | tf_op jit(solution)/shard_map/pallas_call | solution.py:420

commit v6 on v5

--- a/solution.py
+++ b/solution.py
@@ -82,8 +82,7 @@
             (depth_mask_hbm, depth_mask), (column_mask_hbm, column_mask), (row_mask_hbm, row_mask),
         ))
     ]
-    for load in loads:
-        load.start()
+    loads[0].start()
 
     def y_peer(step):
         return chan, lax.rem(y + step, Y) * ring + inner
@@ -118,6 +117,9 @@
                 barrier, inc=1, device_id=(there, y * ring + z_lo * CORES + other), device_id_type=MESH
             )
             greeted += 1
+
+    for load in loads[1:]:
+        load.start()
 
     pick = onehot((seqs, width), same, lambda c: c // 2).astype(BF16)
     even = jnp.where(iota((1, width), 1) % 2 == 0, 1.0, 0.0).astype(BF16)

time: 134 us -> 134 us (level)
  no operation moved by 1% of the time
where the time goes in v6:
time: 134 us
  Pallas kernels  134 us (100%)
    pallas_call x1, Pallas kernels, per_device(): pl.pallas_call(functools.partial(kernel, seqs, outer), out_shape=shapes,...  132 us

profile of v6, /device:TPU:1, one launch (start us, length us, event | category | flops | bytes accessed | tf_op | source)
XLA Modules:
  0.0 134.3 jit_solution(12600535988944731802)
XLA Ops:
  0.6 132.1 %shard_map.103 = (f32[64,64]{1,0:T(8,128)}, f32[64,64]{1,0:T(8,128)}, f32[128,128]{1,0:T(8,128)}) custom-call(bf16[8192,128]{1,0:T(8,128)(2,1)} %signal_hbm.1, bf16[8192,128]{1,0:T(8,128)(2,1)} %cotangent_hbm.1, bf16[64,64]{1,0:T(8,128)(2,1)} %depth_hbm.1, bf16[64,64]{1,0:T(8,128)(2,1)} %column_hbm.1, bf16[128,128]{1,0:T(8,128)(2,1)} %row_hbm.1, ...), custom_call_target="tpu_custom_call" | custom-call | flops 1300000000 | bytes 4194304 | tf_op jit(solution)/shard_map/pallas_call | solution.py:376
  132.7 1.6 %shard_map.104 = (f32[64,64]{1,0:T(8,128)}, f32[64,64]{1,0:T(8,128)}, f32[128,128]{1,0:T(8,128)}) custom-call(f32[64,64]{1,0:T(8,128)} %get-tuple-element.6.refs_0_, f32[64,64]{1,0:T(8,128)} %get-tuple-element.7.refs_1_, f32[128,128]{1,0:T(8,128)} %get-tuple-element.8.refs_2_), custom_call_target="tpu_custom_call" | custom-call | tf_op jit(solution)/shard_map/pallas_call | solution.py:422
